TPU v7x, 32 devices: a whole 2x2x4 slice. The times are simulated.
32 devices in a mesh: src: 8 (over z, core), dst: 4 (over y, x).
Axes of the slice: x: 2, y: 2, z: 4, core: 2. Of those that a mesh axis runs over, the one named last changes fastest.
Arguments:
- adjacency: float32 [5120, 5120], P('dst', 'src'), may hold values from -0.125 to 0.125
- features: float32 [5120, 256], P(('src', 'dst')), may hold values from -6 to 6
- layer_weights: float32 [2, 2, 256, 256], replicated, may hold values from -0.375 to 0.375
- layer_biases: float32 [2, 256], replicated, may hold values from -3 to 3
Outputs:
- result: float32 [5120, 256], P(('src', 'dst'))
All inputs are finite; a program needn't handle non-finite values.
Results may differ from a plain program's by a relative error of at most 0.0001.
Values sent between devices are 32-bit elements; how exact they have to be, the bound alone decides.
A program may use at most 128 MiB of HBM per device.

v0:
```python
import jax
import jax.numpy as jnp
from jax import lax
from jax.sharding import PartitionSpec as P

LAYERS = 2


def broadcast(value, axis, source):
    kept = jnp.where(lax.axis_index(axis) == source, value, 0).astype(value.dtype)
    return lax.psum(kept, axis)


def combine_layer(forward, reverse, weight_in, weight_out, offset_bias):
    mixed = jnp.dot(
        forward, weight_in, precision=lax.Precision.HIGHEST, preferred_element_type=jnp.float32
    )
    mixed = mixed + jnp.dot(
        reverse, weight_out, precision=lax.Precision.HIGHEST, preferred_element_type=jnp.float32
    )
    return jax.nn.relu(mixed + offset_bias[None, :])


def body(adjacency, features, layer_weights, layer_biases):
    own_rows = features.shape[0]
    block_rows = adjacency.shape[1]
    group_ratio = lax.axis_size("src") // lax.axis_size("dst")
    src_index = lax.axis_index("src")
    dst_index = lax.axis_index("dst")
    share_start = dst_index * own_rows
    source_rows = lax.all_gather(features, "dst", axis=0, tiled=True)
    output_rows = features
    for layer_index in range(LAYERS):
        final_layer = layer_index + 1 == LAYERS
        weight_in = layer_weights[layer_index, 0]
        weight_out = layer_weights[layer_index, 1]
        offset_bias = layer_biases[layer_index]
        pieces = []
        for part_index in range(group_ratio):
            pieces.append(broadcast(source_rows, "src", dst_index * group_ratio + part_index))
        dest_rows = jnp.concatenate(pieces, axis=0)
        partial_rows = jnp.dot(
            adjacency,
            source_rows,
            precision=lax.Precision.HIGHEST,
            preferred_element_type=jnp.float32,
        )
        forward_all = lax.psum(partial_rows, "src")
        within = src_index % group_ratio * block_rows
        forward_own = lax.dynamic_slice_in_dim(forward_all, within, block_rows, 0)
        forward_src = broadcast(forward_own, "dst", src_index // group_ratio)
        partial_cols = lax.dot_general(
            adjacency,
            dest_rows,
            (((0,), (0,)), ((), ())),
            precision=lax.Precision.HIGHEST,
            preferred_element_type=jnp.float32,
        )
        reverse_src = lax.psum(partial_cols, "dst")
        if final_layer:
            forward_share = lax.dynamic_slice_in_dim(forward_src, share_start, own_rows, 0)
            reverse_share = lax.dynamic_slice_in_dim(reverse_src, share_start, own_rows, 0)
            output_rows = combine_layer(
                forward_share, reverse_share, weight_in, weight_out, offset_bias
            )
        else:
            source_rows = combine_layer(
                forward_src, reverse_src, weight_in, weight_out, offset_bias
            )
    return output_rows


def solution(mesh):
    placed = (P("dst", "src"), P(("src", "dst"), None), P(), P())
    return jax.shard_map(
        body, mesh=mesh, in_specs=placed, out_specs=P(("src", "dst"), None), check_vma=False
    )
```

profile of v0, /device:TPU:0, one launch (start us, length us, event | category | flops | bytes accessed | tf_op | source)
XLA Modules:
  0.0 309.8 jit_solution(11089945646821713630)
XLA Ops:
  6.5 0.0 copy-start
  6.5 0.0 all-reduce.11.cloned.1.call-start
  6.5 13.0 %all_gather.3 = f32[640,256]{1,0:T(8,128)S(1)} all-gather(f32[160,256]{1,0:T(8,128)} %param.5), channel_id=1, replica_groups=mesh['src'=8,'dst'=4] {'dst'}, dimensions={0}, use_global_device_ids=true | all-gather | bytes 819200 | tf_op jit(solution)/shard_map/all_gather | solution.py:31
  19.5 0.0 copy-done
  19.5 4.3 %fusion.35 = f32[1280,256]{1,0:T(8,128)} fusion(f32[1280,640]{1,0:T(8,128)S(1)} %copy-done, f32[640,256]{1,0:T(8,128)S(1)} %all_gather.3), kind=kOutput, calls=%fused_computation.40 | convolution fusion | flops 2516582400 | bytes 5242880 | tf_op jit(solution)/shard_map/dot_general | solution.py:42
  23.9 1.2 broadcast_select_fusion.3
  25.0 0.0 all-reduce.11.cloned.1.call-update
  25.0 0.0 all-reduce.15.cloned.1.call-start
  25.1 69.9 %all-reduce.11.cloned.1.call-done = (f32[1280,256]{1,0:T(8,128)}, f32[640,256]{1,0:T(8,128)}, f32[640,256]{1,0:T(8,128)}) async-done(((f32[1280,256]{1,0:T(8,128)}, f32[640,256]{1,0:T(8,128)}, f32[640,256]{1,0:T(8,128)}), (f32[1280,256]{1,0:T(8,128)}, f32[640,256]{1,0:T(8,128)}, f32[640,256]{1,0:T(8,128)})) %all-reduce.11.cloned.1.call-update) | async-done | bytes 2621456 | tf_op jit(solution)/shard_map/psum | solution.py:48
  95.0 0.0 copy-start.4
  95.0 5.6 %fusion.11 = f32[640,256]{0,1:T(8,128)} fusion(f32[1280,640]{1,0:T(8,128)S(1)} %copy-done, f32[640,256]{1,0:T(8,128)} %get-tuple-element.9, f32[640,256]{1,0:T(8,128)} %get-tuple-element.10), kind=kOutput, calls=%fused_computation.10 | convolution fusion | flops 2516910080 | bytes 5242880 | tf_op jit(solution)/shard_map/dot_general | solution.py:52
  100.6 0.0 copy-done.4
  100.6 0.9 dynamic-slice_select_fusion.1
  101.5 0.0 all-reduce.15.cloned.1.call-update
  101.6 0.2 all-reduce.9.cloned.1.call-start
  101.8 0.0 copy-done.5
  101.8 55.7 %all-reduce.15.cloned.1.call-done = (f32[640,256]{1,0:T(8,128)}, f32[640,256]{0,1:T(8,128)}) async-done(((f32[640,256]{1,0:T(8,128)}, f32[640,256]{0,1:T(8,128)}), (f32[640,256]{1,0:T(8,128)}, f32[640,256]{0,1:T(8,128)})) %all-reduce.15.cloned.1.call-update) | async-done | bytes 1310736 | tf_op jit(solution)/shard_map/psum | solution.py:11
  157.5 1.9 fusion.22
  159.4 0.0 copy-done.3
  159.4 3.2 %broadcast_select_fusion.1 = (f32[640,256]{1,0:T(8,128)}, f32[640,256]{1,0:T(8,128)}, f32[640,256]{1,0:T(8,128)S(1)}) fusion(pred[]{:T(512)S(6)} %eq.16, pred[]{:T(512)S(6)} %eq.17, f32[256]{0:T(256)S(1)} %bitcast.31, f32[640,256]{1,0:T(8,128)S(1)} %fusion.22, f32[640,256]{0,1:T(8,128)S(1)} %copy-done.3, f32[2,2,256,256]{3,2,1,0:T(8,128)} %param.6), kind=kOutput, calls=%fused_computation.20 | convolution fusion | flops 504135680 | bytes 3539970 | tf_op jit(solution)/shard_map/dot_general | solution.py:18
  162.7 4.3 %convolution_bitcast_fusion = f32[1280,256]{1,0:T(8,128)} fusion(f32[640,256]{1,0:T(8,128)S(1)} %get-tuple-element.21, f32[1280,640]{1,0:T(8,128)S(1)} %copy-done), kind=kOutput, calls=%fused_computation | convolution fusion | flops 2516582400 | bytes 5242880 | tf_op jit(solution)/shard_map/dot_general | solution.py:42
  167.0 0.0 all-reduce.9.cloned.1.call-update
  167.0 0.0 all-reduce.13.cloned.1.call-start
  167.1 69.9 %all-reduce.9.cloned.1.call-done = (f32[1280,256]{1,0:T(8,128)}, f32[640,256]{1,0:T(8,128)}, f32[640,256]{1,0:T(8,128)}) async-done(((f32[1280,256]{1,0:T(8,128)}, f32[640,256]{1,0:T(8,128)}, f32[640,256]{1,0:T(8,128)}), (f32[1280,256]{1,0:T(8,128)}, f32[640,256]{1,0:T(8,128)}, f32[640,256]{1,0:T(8,128)})) %all-reduce.9.cloned.1.call-update) | async-done | bytes 2621456 | tf_op jit(solution)/shard_map/psum | solution.py:48
  237.0 2.1 dynamic-slice_select_fusion
  239.0 0.0 copy-done.1
  239.0 0.0 copy-done.2
  239.0 4.5 %fusion.8 = f32[640,256]{0,1:T(8,128)} fusion(f32[1280,640]{1,0:T(8,128)S(1)} %copy-done, f32[640,256]{1,0:T(8,128)S(1)} %copy-done.1, f32[640,256]{1,0:T(8,128)S(1)} %copy-done.2), kind=kOutput, calls=%fused_computation.9 | convolution fusion | flops 2516910080 | bytes 5242880 | tf_op jit(solution)/shard_map/dot_general | solution.py:52
  243.5 0.0 all-reduce.13.cloned.1.call-update
  243.6 56.0 %all-reduce.13.cloned.1.call-done = (f32[640,256]{1,0:T(8,128)}, f32[640,256]{0,1:T(8,128)}) async-done(((f32[640,256]{1,0:T(8,128)}, f32[640,256]{0,1:T(8,128)}), (f32[640,256]{1,0:T(8,128)}, f32[640,256]{0,1:T(8,128)})) %all-reduce.13.cloned.1.call-update) | async-done | bytes 1310736 | tf_op jit(solution)/shard_map/psum | solution.py:11
  299.5 1.3 fusion.19
  300.9 2.4 fusion.17
  (5 shorter events, 0.0 us)
Async XLA Ops:
  6.5 13.0 %copy-start = (f32[1280,640]{1,0:T(8,128)S(1)}, f32[1280,640]{1,0:T(8,128)}, u32[]{:S(2)}) copy-start(f32[1280,640]{1,0:T(8,128)} %param.4) | copy-start | bytes 9830404
  6.5 88.5 %all-reduce.11.cloned.1.call-start = ((), (), s32[]{:S(2)}) async-start(), calls=%async_computation.1 | async-start | bytes 5242880 | tf_op jit(solution)/shard_map/psum | solution.py:48
  25.0 132.5 %all-reduce.15.cloned.1.call-start = ((), (), s32[]{:S(2)}) async-start(), calls=%async_computation.3 | async-start | bytes 2621440 | tf_op jit(solution)/shard_map/psum | solution.py:11
  95.0 5.6 %copy-start.4 = (f32[1280,256]{1,0:T(8,128)S(1)}, f32[1280,256]{1,0:T(8,128)}, u32[]{:S(2)}) copy-start(f32[1280,256]{1,0:T(8,128)} %get-tuple-element.8) | copy-start | bytes 3932164
  100.6 1.2 copy-start.5
  101.6 135.4 %all-reduce.9.cloned.1.call-start = ((), (), s32[]{:S(2)}) async-start(), calls=%async_computation | async-start | bytes 5242880 | tf_op jit(solution)/shard_map/psum | solution.py:48
  157.5 1.9 copy-start.3
  167.0 132.5 %all-reduce.13.cloned.1.call-start = ((), (), s32[]{:S(2)}) async-start(), calls=%async_computation.2 | async-start | bytes 2621440 | tf_op jit(solution)/shard_map/psum | solution.py:11
  237.0 2.1 copy-start.1
  237.0 2.1 copy-start.2
Sparse Core Ops, SparseCore 0:
  25.2 69.7 all-reduce.10
  101.7 55.8 all-reduce.14
  167.2 69.7 all-reduce.8
  243.7 55.8 all-reduce.12
where the time goes:
time: 310 us
  waiting for transfers between devices  252 us (81%)
  matrix products  27.7 us (9%)
  between operations  13.2 us (4%)
  blocking collectives  13 us (4%)
  other arithmetic  4.13 us (1%)
    psum x2, waiting for transfers between devices, body(): forward_all = lax.psum(partial_rows, 'src')  140 us
    psum x2, waiting for transfers between devices, broadcast(): return lax.psum(kept, axis)  112 us
    all_gather x1, blocking collectives, body(): source_rows = lax.all_gather(features, 'dst', axis=0, tiled=True)  13 us
    dot_general x2, matrix products, body(): lax.dot_general(adjacency, dest_rows, (((0,), (0,)), ((), ())), precision...  10.1 us
    dot_general x2, matrix products, body(): jnp.dot(adjacency, source_rows, precision=lax.Precision.HIGHEST, preferre...  8.65 us
  transfers between devices with their start and end apart: 4, of which 4 were waited for; matrix products, arithmetic and copies ran while one was open for 0% of the time, Pallas kernels for 0%

commit v1 on v0

v1 whole, which is shorter than its diff:
```python
import jax
import jax.numpy as jnp
from jax import lax
from jax.sharding import PartitionSpec as P

HIGH = lax.Precision.HIGH


def matmul(a, b, dims=(((1,), (0,)), ((), ()))):
    return lax.dot_general(a, b, dims, precision=HIGH, preferred_element_type=jnp.float32)


def body(adjacency, features, layer_weights, layer_biases):
    n_src, n_dst = lax.axis_size("src"), lax.axis_size("dst")
    owner = [(g, (g % n_src) * n_dst + g // n_src) for g in range(n_src * n_dst)]
    back = [(b, a) for a, b in owner]
    rows = features
    for layer in range(layer_weights.shape[0]):
        share = lax.ppermute(rows, ("src", "dst"), owner)
        source_rows = lax.all_gather(rows, "dst", axis=0, tiled=True)
        dest_rows = lax.all_gather(share, "src", axis=0, tiled=True)
        partial_rows = matmul(adjacency, source_rows)
        forward = lax.psum_scatter(partial_rows, "src", scatter_dimension=0, tiled=True)
        forward = lax.ppermute(forward, ("src", "dst"), back)
        partial_cols = matmul(adjacency, dest_rows, (((0,), (0,)), ((), ())))
        reverse = lax.psum_scatter(partial_cols, "dst", scatter_dimension=0, tiled=True)
        mixed = matmul(forward, layer_weights[layer, 0]) + matmul(reverse, layer_weights[layer, 1])
        rows = jax.nn.relu(mixed + layer_biases[layer][None, :])
    return rows


def solution(mesh):
    placed = (P("dst", "src"), P(("src", "dst"), None), P(), P())
    return jax.shard_map(
        body, mesh=mesh, in_specs=placed, out_specs=P(("src", "dst"), None), check_vma=False
    )
```

time: 310 us -> 221 us (0.71)
  waiting for transfers between devices: 252 us -> 126 us
  blocking collectives: 13 us -> 45.1 us
  local copies, waits for them, and re-layouts: 0.03 us -> 7.36 us
  matrix products: 27.7 us -> 21.6 us
  starting transfers between devices: 0.31 us -> 6.34 us
  other arithmetic: 4.13 us -> 0 us
    psum x4 -> x0, waiting for transfers between devices: 251 us -> none  [the longest x2 140 us: body(): forward_all = lax.psum(partial_rows, 'src')]
    reduce_scatter x0 -> x2, waiting for transfers between devices: none -> 57 us  [the longest x1 30.1 us: body(): lax.psum_scatter(partial_rows, 'src', scatter_dimension=0, tiled=True)]
    unnamed x4 -> x8, waiting for transfers between devices: 0.07 us -> 55.6 us
    all_gather x1 -> x2, blocking collectives: 13 us -> 45.1 us  [body(): source_rows = lax.all_gather(rows, 'dst', axis=0, tiled=True)]
    all_gather x0 -> x2, waiting for transfers between devices: none -> 13.8 us  [body(): dest_rows = lax.all_gather(share, 'src', axis=0, tiled=True)]
    unnamed x12 -> x11, local copies, waits for them, and re-layouts: 0.02 us -> 7.35 us
    ppermute x0 -> x4, starting transfers between devices: none -> 6.13 us  [the longest x2 3.21 us: body(): share = lax.ppermute(rows, ('src', 'dst'), owner)]
    dot_general x8, matrix products: 27.7 us -> 21.6 us  [matmul(): lax.dot_general(a, b, dims, precision=HIGH, preferred_element_type=jnp.fl...]
  transfers between devices with their start and end apart: 4 -> 10, of which waited for: 4 -> 6; matrix products, arithmetic and copies ran while one was open for 0% -> 11% of each run, Pallas kernels for 0% -> 0%
where the time goes in v1:
time: 221 us; the launch traced here: 220 us
  waiting for transfers between devices  126 us (57%)
  blocking collectives  45.1 us (20%)
  matrix products  21.6 us (10%)
  between operations  13.6 us (6%)
  local copies, waits for them, and re-layouts  7.36 us (3%)
  starting transfers between devices  6.34 us (3%)
    unnamed x8, waiting for transfers between devices  55.6 us
    all_gather x2, blocking collectives, body(): source_rows = lax.all_gather(rows, 'dst', axis=0, tiled=True)  45.1 us
    reduce_scatter x1, waiting for transfers between devices, body(): lax.psum_scatter(partial_rows, 'src', scatter_dimension=0, tiled=True)  30.1 us
    reduce_scatter x1, waiting for transfers between devices, body(): lax.psum_scatter(partial_cols, 'dst', scatter_dimension=0, tiled=True)  26.9 us
    dot_general x8, matrix products, matmul(): lax.dot_general(a, b, dims, precision=HIGH, preferred_element_type=jnp.fl...  21.6 us
    all_gather x2, waiting for transfers between devices, body(): dest_rows = lax.all_gather(share, 'src', axis=0, tiled=True)  13.8 us
    unnamed x11, local copies, waits for them, and re-layouts  7.35 us
  transfers between devices with their start and end apart: 10, of which 6 were waited for; matrix products, arithmetic and copies ran while one was open for 11% of the time, Pallas kernels for 0%

profile of v1, /device:TPU:0, one launch (start us, length us, event | category | flops | bytes accessed | tf_op | source)
XLA Modules:
  0.0 220.4 jit_solution(12772999181238431601)
XLA Ops:
  6.5 1.9 collective-permute-start.1
  8.4 0.7 copy-done.1
  9.1 0.0 all-gather.3.cloned.1.call-update
  9.1 0.0 reduce-scatter.9.cloned.1.call-start
  9.2 23.6 %all_gather.12 = f32[640,256]{1,0:T(8,128)S(1)} all-gather(f32[160,256]{1,0:T(8,128)} %param.5), channel_id=1, replica_groups=mesh['src'=8,'dst'=4] {'dst'}, dimensions={0}, use_global_device_ids=true | all-gather | bytes 819200 | tf_op jit(solution)/shard_map/all_gather | solution.py:20
  32.8 2.8 %fusion.15 = f32[1280,256]{1,0:T(8,128)} fusion(f32[1280,640]{1,0:T(8,128)S(1)} %copy-done, f32[640,256]{1,0:T(8,128)S(1)} %all_gather.12), kind=kOutput, calls=%fused_computation.19 | convolution fusion | flops 1258291200 | bytes 5242880 | tf_op jit(solution)/shard_map/dot_general | solution.py:10
  35.6 0.0 reduce-scatter.11.cloned.1.call-start
  35.7 8.6 %all-gather.3.cloned.1.call-done = f32[1280,256]{1,0:T(8,128)} async-done(((f32[160,256]{1,0:T(8,128)}), f32[1280,256]{1,0:T(8,128)}) %all-gather.3.cloned.1.call-update) | async-done | bytes 1310736 | tf_op jit(solution)/shard_map/all_gather | solution.py:21
  44.3 4.9 %fusion.16 = f32[640,256]{1,0:T(8,128)} fusion(f32[1280,640]{1,0:T(8,128)S(1)} %copy-done, f32[1280,256]{1,0:T(8,128)} %all-gather.3.cloned.1.call-done), kind=kOutput, calls=%fused_computation.20 | convolution fusion | flops 1258291200 | bytes 5242880 | tf_op jit(solution)/shard_map/dot_general | solution.py:10
  49.2 0.0 all-gather.5.cloned.1.call-start
  49.3 30.1 %reduce-scatter.9.cloned.1.call-done = f32[160,256]{1,0:T(8,128)} async-done(((f32[1280,256]{1,0:T(8,128)}), f32[160,256]{1,0:T(8,128)}) %reduce-scatter.9.cloned.1.call-update) | async-done | bytes 163856 | tf_op jit(solution)/shard_map/reduce_scatter | solution.py:23
  79.4 1.6 collective-permute-start
  81.0 26.9 %reduce-scatter.11.cloned.1.call-done = f32[160,256]{1,0:T(8,128)} async-done(((f32[640,256]{1,0:T(8,128)}), f32[160,256]{1,0:T(8,128)}) %reduce-scatter.11.cloned.1.call-update) | async-done | bytes 163856 | tf_op jit(solution)/shard_map/reduce_scatter | solution.py:26
  107.8 1.3 fusion.7
  109.1 0.7 copy-done.2
  109.8 1.3 fusion.3
  111.1 1.3 collective-permute-start.3
  112.4 0.0 all-gather.5.cloned.1.call-update
  112.4 0.0 reduce-scatter.13.cloned.1.call-start
  112.5 21.5 %all_gather.14 = f32[640,256]{1,0:T(8,128)S(1)} all-gather(f32[160,256]{1,0:T(8,128)S(1)} %fusion.3), channel_id=1, replica_groups=mesh['src'=8,'dst'=4] {'dst'}, dimensions={0}, use_global_device_ids=true | all-gather | bytes 819200 | tf_op jit(solution)/shard_map/all_gather | solution.py:20
  133.9 4.0 %convolution_bitcast_fusion = f32[1280,256]{0,1:T(8,128)} fusion(f32[640,256]{1,0:T(8,128)S(1)} %all_gather.14, f32[1280,640]{1,0:T(8,128)S(1)} %copy-done), kind=kOutput, calls=%fused_computation | convolution fusion | flops 1258291200 | bytes 5242880 | tf_op jit(solution)/shard_map/dot_general | solution.py:10
  137.9 2.8 %copy.5 = f32[1280,256]{1,0:T(8,128)} copy(f32[1280,256]{0,1:T(8,128)} %convolution_bitcast_fusion) | data formatting | bytes 2621440
  140.7 0.0 reduce-scatter.15.cloned.1.call-start
  140.8 5.2 %all-gather.5.cloned.1.call-done = f32[1280,256]{1,0:T(8,128)} async-done(((f32[160,256]{1,0:T(8,128)}), f32[1280,256]{1,0:T(8,128)}) %all-gather.5.cloned.1.call-update) | async-done | bytes 1310736 | tf_op jit(solution)/shard_map/all_gather | solution.py:21
  146.0 4.1 %convolution_bitcast_fusion.1 = f32[640,256]{0,1:T(8,128)} fusion(f32[1280,256]{1,0:T(8,128)} %all-gather.5.cloned.1.call-done, f32[1280,640]{1,0:T(8,128)S(1)} %copy-done), kind=kOutput, calls=%fused_computation.1 | convolution fusion | flops 1258291200 | bytes 5242880 | tf_op jit(solution)/shard_map/dot_general | solution.py:10
  150.0 2.2 copy.7
  152.2 28.7 %reduce-scatter.13.cloned.1.call-done = f32[160,256]{1,0:T(8,128)} async-done(((f32[1280,256]{1,0:T(8,128)}), f32[160,256]{1,0:T(8,128)}) %reduce-scatter.13.cloned.1.call-update) | async-done | bytes 163856
  181.0 1.0 copy.6
  182.0 1.4 collective-permute-start.2
  183.4 26.8 %reduce-scatter.15.cloned.1.call-done = f32[160,256]{1,0:T(8,128)} async-done(((f32[640,256]{1,0:T(8,128)}), f32[160,256]{1,0:T(8,128)}) %reduce-scatter.15.cloned.1.call-update) | async-done | bytes 163856
  210.2 1.3 fusion.4
  211.5 2.1 fusion.1
  (16 shorter events, 0.1 us)
Async XLA Ops:
  6.5 26.3 %copy-start = (f32[1280,640]{1,0:T(8,128)S(1)}, f32[1280,640]{1,0:T(8,128)}, u32[]{:S(2)}) copy-start(f32[1280,640]{1,0:T(8,128)} %param.4) | copy-start | bytes 9830404
  6.5 37.8 %all-gather.3.cloned.1.call-start = ((), (), s32[]{:S(2)}) async-start(), calls=%async_computation.5 | async-start | bytes 1474560 | tf_op jit(solution)/shard_map/all_gather | solution.py:21
  6.5 1.9 collective-permute-start.1
  8.4 0.7 copy-start.1
  9.1 70.3 %reduce-scatter.9.cloned.1.call-start = ((), (), s32[]{:S(2)}) async-start(), calls=%async_computation.4 | async-start | bytes 1474560 | tf_op jit(solution)/shard_map/reduce_scatter | solution.py:23
  35.6 13.7 %copy-start.3 = (f32[2,256]{1,0:T(2,128)S(1)}, f32[2,256]{1,0:T(2,128)}, u32[]{:S(2)}) copy-start(f32[2,256]{1,0:T(2,128)} %param.7) | copy-start | bytes 6148
  35.6 72.2 %reduce-scatter.11.cloned.1.call-start = ((), (), s32[]{:S(2)}) async-start(), calls=%async_computation.6 | async-start | bytes 819200 | tf_op jit(solution)/shard_map/reduce_scatter | solution.py:26
  49.2 96.7 %all-gather.5.cloned.1.call-start = ((), (), s32[]{:S(2)}) async-start(), calls=%async_computation.7 | async-start | bytes 1474560 | tf_op jit(solution)/shard_map/all_gather | solution.py:21
  79.4 29.7 %collective-permute-start = (f32[160,256]{1,0:T(8,128)}, f32[160,256]{1,0:T(8,128)S(1)}, u32[]{:S(2)}, u32[]{:S(2)}) collective-permute-start(f32[160,256]{1,0:T(8,128)} %reduce-scatter.9.cloned.1.call-done), channel_id=1, source_target_pairs={{0,0},{4,1},{8,2},{12,3},{16,4},{20,5},{24,6},{28,7},{1,8},{5,9},{... | collective-permute-start | bytes 491528 | tf_op jit(solution)/shard_map/ppermute | solution.py:24
  109.1 0.7 copy-start.2
  111.1 1.3 collective-permute-start.3
  112.4 68.6 %reduce-scatter.13.cloned.1.call-start = ((), (), s32[]{:S(2)}) async-start(), calls=%async_computation.8 | async-start | bytes 1474560
  140.7 69.4 %reduce-scatter.15.cloned.1.call-start = ((), (), s32[]{:S(2)}) async-start(), calls=%async_computation.9 | async-start | bytes 819200
  182.0 29.4 %collective-permute-start.2 = (f32[160,256]{0,1:T(8,128)S(1)}, f32[160,256]{0,1:T(8,128)}, u32[]{:S(2)}, u32[]{:S(2)}) collective-permute-start(f32[160,256]{0,1:T(8,128)S(1)} %copy.6), channel_id=1, source_target_pairs={{0,0},{4,1},{8,2},{12,3},{16,4},{20,5},{24,6},{28,7},{1,8},{5,9},{... | collective-permute-start | bytes 491528 | tf_op jit(solution)/shard_map/ppermute | solution.py:24
Sparse Core Ops, SparseCore 0:
  9.3 35.0 all-gather.2
  46.6 32.7 reduce-scatter.8
  82.3 25.5 reduce-scatter.10
  112.5 33.3 all-gather.4
  148.2 32.7 reduce-scatter.12
  184.0 26.1 reduce-scatter.14

commit v2 on v1

v2 whole, which is shorter than its diff:
```python
import functools

import jax
import jax.numpy as jnp
from jax import lax
from jax.experimental import pallas as pl
from jax.experimental.pallas import tpu as pltpu
from jax.sharding import PartitionSpec as P

MESH = pl.DeviceIdType.MESH
CORES = 2
SPLIT = 2


def parts_of(value):
    high = value.astype(jnp.bfloat16)
    return high, (value - high.astype(jnp.float32)).astype(jnp.bfloat16)


def dot3(a_high, a_low, b_high, b_low):
    dot = functools.partial(jnp.dot, preferred_element_type=jnp.float32)
    return dot(a_high, b_high) + (dot(a_high, b_low) + dot(a_low, b_high))


def kernel(
    n, layers, tile,
    adj, feat, weights, biases, out,
    stage, a_hi, a_lo, t_hi, t_lo, xs_hi, xs_lo,
    xs, xd, swap_out, own, rev, pair_in, chain_in, rev_in, total_in,
    load_sem, gs, gr, zs, zr, cs, cr, ps, pr, hs, hr, fs, fr, vs, vr,
):
    rows, width = feat.shape
    half = n * rows
    chunk = rows // SPLIT
    chunks = n * SPLIT
    tiles = CORES * half // tile
    s, d = lax.axis_index("src"), lax.axis_index("dst")
    u, c = lax.div(s, CORES), lax.rem(s, CORES)
    root = u == d
    below = jnp.logical_and(u <= d, u > 0)
    above = jnp.logical_and(u >= d, u < n - 1)
    distance = jnp.abs(u - d)
    reach = jnp.where(u < d, d, n - 1 - d)
    lag = jnp.where(root, 0, reach - distance)
    mate = {"src": u * CORES + 1 - c, "dst": d}
    down = {"src": s - CORES, "dst": d}
    up = {"src": s + CORES, "dst": d}
    inward = {"src": jnp.where(u < d, s + CORES, s - CORES), "dst": d}
    side = jnp.where(u < d, 0, 1)

    def peer(j):
        return {"src": s, "dst": lax.rem(d + j, n)}

    def span(start, size):
        return pl.ds(pl.multiple_of(start, size), size)

    def remote(src, dst, send, recv, device):
        return pltpu.make_async_remote_copy(
            src_ref=src, dst_ref=dst, send_sem=send, recv_sem=recv,
            device_id=device, device_id_type=MESH,
        )

    def load(t, slot):
        return pltpu.make_async_copy(adj.at[span(t * tile, tile)], stage.at[slot], load_sem.at[slot])

    load(0, 0).start()
    if tiles > 1:
        load(1, 1).start()

    barrier = pltpu.get_barrier_semaphore()
    for j in range(1, n):
        pl.semaphore_signal(barrier, inc=1, device_id=peer(j), device_id_type=MESH)
    pl.semaphore_signal(barrier, inc=1, device_id=mate, device_id_type=MESH)

    @pl.when(u > 0)
    def _():
        pl.semaphore_signal(barrier, inc=1, device_id=down, device_id_type=MESH)

    @pl.when(u < n - 1)
    def _():
        pl.semaphore_signal(barrier, inc=1, device_id=up, device_id_type=MESH)

    xs[0, span(d * rows, rows)] = feat[...]
    pl.semaphore_wait(barrier, n + (u > 0).astype(jnp.int32) + (u < n - 1).astype(jnp.int32))

    def prepare():
        def step(t, carry):
            slot = lax.rem(t, 2)
            load(t, slot).wait()
            block = stage[slot]
            high, low = parts_of(block)
            a_hi[span(t * tile, tile)] = high
            a_lo[span(t * tile, tile)] = low
            turned_high, turned_low = parts_of(block.T)
            t_hi[t] = turned_high
            t_lo[t] = turned_low

            @pl.when(t + 2 < tiles)
            def _():
                load(t + 2, slot).start()

            return carry

        lax.fori_loop(0, tiles, step, 0)

    for l in range(layers):

        def gather(j):
            own_rows = xs.at[l, span(d * rows, rows)]
            return remote(own_rows, own_rows, gs.at[l, j], gr.at[l, n - j], peer(j))

        def gathered(i):
            rows_of = xs.at[l, span(lax.rem(d + i, n) * rows, rows)]
            return remote(rows_of, rows_of, gs.at[l, i], gr.at[l, i], peer(i))

        def place(k):
            group = lax.rem(d + lax.div(k, SPLIT), n)
            return group * rows + lax.rem(k, SPLIT) * chunk

        def spread(k, to, device):
            ref = xd.at[l, span(c * half + place(k), chunk)]
            return remote(ref, ref, zs.at[l, to, k], zr.at[l, k], device)

        def share(k):
            ref = xd.at[l, span(c * half + place(k), chunk)]
            return remote(ref, ref, cs.at[l, k], cr.at[l, k], mate)

        def spread_group(g):
            for part in range(SPLIT):
                k = g * SPLIT + part

                @pl.when(root)
                def _():
                    xd[l, span(c * half + place(k), chunk)] = xs[l, span(place(k), chunk)]

                @pl.when(jnp.logical_not(root))
                def _():
                    spread(k, 0, down).wait_recv()

                @pl.when(below)
                def _():
                    spread(k, 0, down).start()

                @pl.when(above)
                def _():
                    spread(k, 1, up).start()

                share(k).start()

        def pair(k):
            span_k = span(k * chunk, chunk)
            return remote(swap_out.at[span_k], pair_in.at[l, span_k], ps.at[l, k], pr.at[l, k], mate)

        def chain(k, which):
            span_k = span(k * chunk, chunk)
            return remote(
                own.at[span_k], chain_in.at[l, which, span_k], hs.at[l, k], hr.at[l, which, k], inward
            )

        def total(r):
            return remote(
                own.at[span(r * rows, rows)], total_in.at[l], fs.at[l, r], fr.at[l], {"src": s, "dst": r}
            )

        def reduce_group(r):
            for part in range(SPLIT):
                k = r * SPLIT + part
                span_k = span(k * chunk, chunk)
                pair(k).wait_recv()
                own[span_k] = own[span_k] + pair_in[l, span_k]

                @pl.when(below)
                def _():
                    chain(k, 0).wait_recv()
                    own[span_k] = own[span_k] + chain_in[l, 0, span_k]

                @pl.when(above)
                def _():
                    chain(k, 1).wait_recv()
                    own[span_k] = own[span_k] + chain_in[l, 1, span_k]

                @pl.when(jnp.logical_not(root))
                def _():
                    chain(k, side).start()

            @pl.when(jnp.logical_and(root, r == d))
            def _():
                total_in[l] = own[span(r * rows, rows)]

            @pl.when(jnp.logical_and(root, r != d))
            def _():
                total(r).start()

        def reverse_out(j):
            rows_of = rev.at[span(lax.rem(d + j, n) * rows, rows)]
            return remote(rows_of, rev_in.at[l, n - j], vs.at[l, j], vr.at[l, n - j], peer(j))

        def reverse():
            def arrive(k, carry):
                share(k).wait_recv()
                return carry

            lax.fori_loop(0, chunks, arrive, 0)
            rev[...] = jnp.zeros_like(rev)

            def step(t, carry):
                x_hi, x_lo = parts_of(xd[l, span(t * tile, tile)])
                rev[...] += dot3(t_hi[t], t_lo[t], x_hi, x_lo)
                return carry

            lax.fori_loop(0, tiles, step, 0)
            for j in range(1, n):
                reverse_out(j).start()

        for j in range(1, n):
            gather(j).start()
        for i in range(n):
            if i > 0:
                gathered(i).wait_recv()

            @pl.when(i >= distance)
            def _():
                spread_group(i - distance)

            if l == 0 and i == 0:
                prepare()

        x_hi, x_lo = parts_of(xs[l])
        xs_hi[...] = x_hi
        xs_lo[...] = x_lo
        strip = half // 2
        strip_chunks = chunks // 2

        def forward(i, carry):
            start = i * strip
            at = span((1 - c) * half + start, strip)
            swap_out[span(start, strip)] = dot3(a_hi[at], a_lo[at], xs_hi[...], xs_lo[...])

            def post(k, inner):
                pair(i * strip_chunks + k).start()
                return inner

            lax.fori_loop(0, strip_chunks, post, 0)
            return carry

        lax.fori_loop(0, 2, forward, 0)

        def forward_own(i, carry):
            start = i * strip
            at = span(c * half + start, strip)
            own[span(start, strip)] = dot3(a_hi[at], a_lo[at], xs_hi[...], xs_lo[...])
            return carry

        lax.fori_loop(0, 2, forward_own, 0)

        def turn(t, carry):
            @pl.when(t < distance)
            def _():
                spread_group(n - distance + t)

            @pl.when(t == distance)
            def _():
                reverse()

            @pl.when(jnp.logical_and(t >= lag, t < lag + n))
            def _():
                reduce_group(t - lag)

            return carry

        lax.fori_loop(0, 2 * n - 1, turn, 0)

        back = rev[span(d * rows, rows)]
        for i in range(1, n):
            remote(
                rev.at[span(d * rows, rows)], rev_in.at[l, i], vs.at[l, i], vr.at[l, i], peer(i)
            ).wait_recv()
            back = back + rev_in[l, i]

        @pl.when(jnp.logical_not(root))
        def _():
            total(d).wait_recv()

        mixed = dot3(*parts_of(total_in[l]), *parts_of(weights[l, 0]))
        mixed = mixed + dot3(*parts_of(back), *parts_of(weights[l, 1]))
        result = jnp.maximum(mixed + biases[pl.ds(l, 1)], 0.0)
        if l + 1 < layers:
            xs[l + 1, span(d * rows, rows)] = result
        else:
            out[...] = result

        for j in range(1, n):
            gather(j).wait_send()
            reverse_out(j).wait_send()

        def drain(k, carry):
            share(k).wait_send()
            pair(k).wait_send()

            @pl.when(below)
            def _():
                spread(k, 0, down).wait_send()

            @pl.when(above)
            def _():
                spread(k, 1, up).wait_send()

            @pl.when(jnp.logical_not(root))
            def _():
                chain(k, side).wait_send()

            return carry

        lax.fori_loop(0, chunks, drain, 0)
        for r in range(n):

            @pl.when(jnp.logical_and(root, r != d))
            def _():
                total(r).wait_send()


def body(adjacency, features, layer_weights, layer_biases):
    n = lax.axis_size("dst")
    assert lax.axis_size("src") == CORES * n
    layers = layer_weights.shape[0]
    rows, width = features.shape
    half = n * rows
    tile = 256
    tiles = CORES * half // tile
    chunks = n * SPLIT
    f32, bf16 = jnp.float32, jnp.bfloat16
    dma = pltpu.SemaphoreType.DMA
    vmem = pltpu.VMEM
    scratch = [
        vmem((2, tile, half), f32),
        vmem((CORES * half, half), bf16),
        vmem((CORES * half, half), bf16),
        vmem((tiles, half, tile), bf16),
        vmem((tiles, half, tile), bf16),
        vmem((half, width), bf16),
        vmem((half, width), bf16),
        vmem((layers, half, width), f32),
        vmem((layers, CORES * half, width), f32),
        vmem((half, width), f32),
        vmem((half, width), f32),
        vmem((half, width), f32),
        vmem((layers, half, width), f32),
        vmem((layers, 2, half, width), f32),
        vmem((layers, n, rows, width), f32),
        vmem((layers, rows, width), f32),
        dma((2,)),
        dma((layers, n)),
        dma((layers, n)),
        dma((layers, 2, chunks)),
        dma((layers, chunks)),
        dma((layers, chunks)),
        dma((layers, chunks)),
        dma((layers, chunks)),
        dma((layers, chunks)),
        dma((layers, chunks)),
        dma((layers, 2, chunks)),
        dma((layers, n)),
        dma((layers,)),
        dma((layers, n)),
        dma((layers, n)),
    ]
    in_vmem = pl.BlockSpec(memory_space=pltpu.VMEM)
    flops = 2 * 3 * 2 * layers * CORES * half * half * width
    return pl.pallas_call(
        functools.partial(kernel, n, layers, tile),
        out_shape=jax.ShapeDtypeStruct((rows, width), f32),
        in_specs=[pl.BlockSpec(memory_space=pl.ANY), in_vmem, in_vmem, in_vmem],
        out_specs=in_vmem,
        scratch_shapes=scratch,
        compiler_params=pltpu.CompilerParams(
            collective_id=0, has_side_effects=True, vmem_limit_bytes=60 * 2**20
        ),
        cost_estimate=pl.CostEstimate(
            flops=flops, bytes_accessed=adjacency.size * 4, transcendentals=0
        ),
    )(adjacency, features, layer_weights, layer_biases)


def solution(mesh):
    placed = (P("dst", "src"), P(("src", "dst"), None), P(), P())
    return jax.shard_map(
        body, mesh=mesh, in_specs=placed, out_specs=P(("src", "dst"), None), check_vma=False
    )
```

time: 221 us -> 103 us (0.47)
  waiting for transfers between devices: 126 us -> 0 us
  Pallas kernels: 0 us -> 101 us
  blocking collectives: 45.1 us -> 0 us
  matrix products: 21.6 us -> 0 us
  between operations: 13.6 us -> 0.01 us
  starting transfers between devices: 6.34 us -> 0 us
  local copies, waits for them, and re-layouts: 7.36 us -> 1.59 us
    pallas_call x0 -> x1, Pallas kernels: none -> 101 us  [body(): pl.pallas_call(functools.partial(kernel, n, layers, tile), out_shape=jax....]
    reduce_scatter x2 -> x0, waiting for transfers between devices: 57 us -> none  [the longest x1 30.1 us: body(): lax.psum_scatter(partial_rows, 'src', scatter_dimension=0, tiled=True)]
    unnamed x8 -> x0, waiting for transfers between devices: 55.6 us -> none
    all_gather x2 -> x0, blocking collectives: 45.1 us -> none  [body(): source_rows = lax.all_gather(rows, 'dst', axis=0, tiled=True)]
    dot_general x8 -> x0, matrix products: 21.6 us -> none  [matmul(): lax.dot_general(a, b, dims, precision=HIGH, preferred_element_type=jnp.fl...]
    all_gather x2 -> x0, waiting for transfers between devices: 13.8 us -> none  [body(): dest_rows = lax.all_gather(share, 'src', axis=0, tiled=True)]
    ppermute x4 -> x0, starting transfers between devices: 6.13 us -> none  [the longest x2 3.21 us: body(): share = lax.ppermute(rows, ('src', 'dst'), owner)]
    unnamed x11 -> x1, local copies, waits for them, and re-layouts: 7.35 us -> 1.59 us
  transfers between devices with their start and end apart: 10 -> 0, of which waited for: 6 -> 0; matrix products, arithmetic and copies ran while one was open for 11% -> 0% of each run, Pallas kernels for 0% -> 0%
where the time goes in v2:
time: 103 us
  Pallas kernels  101 us (98%)
  local copies, waits for them, and re-layouts  1.59 us (2%)
    pallas_call x1, Pallas kernels, body(): pl.pallas_call(functools.partial(kernel, n, layers, tile), out_shape=jax....  101 us

profile of v2, /device:TPU:0, one launch (start us, length us, event | category | flops | bytes accessed | tf_op | source)
XLA Modules:
  0.0 102.7 jit_solution(361006210952302159)
XLA Ops:
  0.0 101.1 %shard_map.46 = f32[160,256]{1,0:T(8,128)} custom-call(f32[1280,640]{1,0:T(8,128)} %adj.1, f32[160,256]{1,0:T(8,128)} %feat.1, f32[2,2,256,256]{3,2,1,0:T(8,128)} %weights.1, f32[2,256]{1,0:T(2,128)} %biases.1), custom_call_target="tpu_custom_call" | custom-call | flops 5033164800 | bytes 3276800 | tf_op jit(solution)/shard_map/pallas_call | solution.py:369
  101.1 1.6 %copy.6 = f32[160,256]{1,0:T(8,128)} copy(f32[160,256]{1,0:T(8,128)} %shard_map.46) | data formatting | bytes 327680

commit v3 on v2

--- a/solution.py
+++ b/solution.py
@@ -41,7 +41,9 @@
     above = jnp.logical_and(u >= d, u < n - 1)
     distance = jnp.abs(u - d)
     reach = jnp.where(u < d, d, n - 1 - d)
-    lag = jnp.where(root, 0, reach - distance)
+    tip = jnp.logical_and(jnp.logical_not(root), distance == reach)
+    lag = jnp.where(jnp.logical_or(root, tip), 0, reach - distance - 1)
+    reverse_turn = jnp.where(root, 0, jnp.where(tip, 2 * n - 1, n - 1))
     mate = {"src": u * CORES + 1 - c, "dst": d}
     down = {"src": s - CORES, "dst": d}
     up = {"src": s + CORES, "dst": d}
@@ -162,7 +164,8 @@
                 own.at[span(r * rows, rows)], total_in.at[l], fs.at[l, r], fr.at[l], {"src": s, "dst": r}
             )
 
-        def reduce_group(r):
+        def reduce_group(i):
+            r = lax.rem(d + 1 + i, n)
             for part in range(SPLIT):
                 k = r * SPLIT + part
                 span_k = span(k * chunk, chunk)
@@ -218,12 +221,16 @@
             if i > 0:
                 gathered(i).wait_recv()
 
-            @pl.when(i >= distance)
-            def _():
-                spread_group(i - distance)
+            @pl.when(root)
+            def _():
+                spread_group(i)
 
             if l == 0 and i == 0:
                 prepare()
+
+        @pl.when(jnp.logical_not(root))
+        def _():
+            spread_group(0)
 
         x_hi, x_lo = parts_of(xs[l])
         xs_hi[...] = x_hi
@@ -254,21 +261,23 @@
         lax.fori_loop(0, 2, forward_own, 0)
 
         def turn(t, carry):
-            @pl.when(t < distance)
-            def _():
-                spread_group(n - distance + t)
-
-            @pl.when(t == distance)
+            @pl.when(t == reverse_turn)
             def _():
                 reverse()
 
+            g = jnp.where(tip, t - n, t) + 1
+
+            @pl.when(jnp.logical_and(jnp.logical_not(root), jnp.logical_and(g >= 1, g < n)))
+            def _():
+                spread_group(g)
+
             @pl.when(jnp.logical_and(t >= lag, t < lag + n))
             def _():
                 reduce_group(t - lag)
 
             return carry
 
-        lax.fori_loop(0, 2 * n - 1, turn, 0)
+        lax.fori_loop(0, 2 * n, turn, 0)
 
         back = rev[span(d * rows, rows)]
         for i in range(1, n):

time: 103 us -> 104 us (level)
    pallas_call x1, Pallas kernels: 101 us -> 102 us  [body(): pl.pallas_call(functools.partial(kernel, n, layers, tile), out_shape=jax....]
where the time goes in v3:
time: 104 us
  Pallas kernels  102 us (98%)
  local copies, waits for them, and re-layouts  1.59 us (2%)
    pallas_call x1, Pallas kernels, body(): pl.pallas_call(functools.partial(kernel, n, layers, tile), out_shape=jax....  102 us

profile of v3, /device:TPU:0, one launch (start us, length us, event | category | flops | bytes accessed | tf_op | source)
XLA Modules:
  0.0 103.8 jit_solution(4539328193744065719)
XLA Ops:
  0.0 102.2 %shard_map.46 = f32[160,256]{1,0:T(8,128)} custom-call(f32[1280,640]{1,0:T(8,128)} %adj.1, f32[160,256]{1,0:T(8,128)} %feat.1, f32[2,2,256,256]{3,2,1,0:T(8,128)} %weights.1, f32[2,256]{1,0:T(2,128)} %biases.1), custom_call_target="tpu_custom_call" | custom-call | flops 5033164800 | bytes 3276800 | tf_op jit(solution)/shard_map/pallas_call | solution.py:378
  102.2 1.6 %copy.6 = f32[160,256]{1,0:T(8,128)} copy(f32[160,256]{1,0:T(8,128)} %shard_map.46) | data formatting | bytes 327680

commit v4 on v3

--- a/solution.py
+++ b/solution.py
@@ -42,8 +42,10 @@
     distance = jnp.abs(u - d)
     reach = jnp.where(u < d, d, n - 1 - d)
     tip = jnp.logical_and(jnp.logical_not(root), distance == reach)
-    lag = jnp.where(jnp.logical_or(root, tip), 0, reach - distance - 1)
-    reverse_turn = jnp.where(root, 0, jnp.where(tip, 2 * n - 1, n - 1))
+    middle = jnp.logical_not(jnp.logical_or(root, tip))
+    reverse_turn = jnp.where(tip, 2 * n + 1, n)
+    spread_turn = jnp.where(tip, n + 1, 0)
+    reduce_turn = jnp.where(root, n, jnp.where(tip, 1, 1 + reach - distance))
     mate = {"src": u * CORES + 1 - c, "dst": d}
     down = {"src": s - CORES, "dst": d}
     up = {"src": s + CORES, "dst": d}
@@ -225,59 +227,51 @@
             def _():
                 spread_group(i)
 
+            @pl.when(jnp.logical_and(middle, distance == i))
+            def _():
+                spread_group(0)
+
             if l == 0 and i == 0:
                 prepare()
-
-        @pl.when(jnp.logical_not(root))
-        def _():
-            spread_group(0)
 
         x_hi, x_lo = parts_of(xs[l])
         xs_hi[...] = x_hi
         xs_lo[...] = x_lo
-        strip = half // 2
-        strip_chunks = chunks // 2
-
-        def forward(i, carry):
-            start = i * strip
-            at = span((1 - c) * half + start, strip)
-            swap_out[span(start, strip)] = dot3(a_hi[at], a_lo[at], xs_hi[...], xs_lo[...])
-
-            def post(k, inner):
-                pair(i * strip_chunks + k).start()
-                return inner
-
-            lax.fori_loop(0, strip_chunks, post, 0)
+
+        def forward(i):
+            start = lax.rem(d + 1 + i, n) * rows
+            at = span((1 - c) * half + start, rows)
+            swap_out[span(start, rows)] = dot3(a_hi[at], a_lo[at], xs_hi[...], xs_lo[...])
+            for part in range(SPLIT):
+                pair(lax.rem(d + 1 + i, n) * SPLIT + part).start()
+            at = span(c * half + start, rows)
+            own[span(start, rows)] = dot3(a_hi[at], a_lo[at], xs_hi[...], xs_lo[...])
+
+        def turn(t, carry):
+            @pl.when(t < n)
+            def _():
+                forward(t)
+
+            @pl.when(t == reverse_turn)
+            def _():
+                reverse()
+
+            g = t - spread_turn
+            first = jnp.where(middle, 1, 0)
+
+            @pl.when(jnp.logical_and(jnp.logical_not(root), jnp.logical_and(g >= first, g < n)))
+            def _():
+                spread_group(g)
+
+            i = t - reduce_turn
+
+            @pl.when(jnp.logical_and(i >= 0, i < n))
+            def _():
+                reduce_group(i)
+
             return carry
 
-        lax.fori_loop(0, 2, forward, 0)
-
-        def forward_own(i, carry):
-            start = i * strip
-            at = span(c * half + start, strip)
-            own[span(start, strip)] = dot3(a_hi[at], a_lo[at], xs_hi[...], xs_lo[...])
-            return carry
-
-        lax.fori_loop(0, 2, forward_own, 0)
-
-        def turn(t, carry):
-            @pl.when(t == reverse_turn)
-            def _():
-                reverse()
-
-            g = jnp.where(tip, t - n, t) + 1
-
-            @pl.when(jnp.logical_and(jnp.logical_not(root), jnp.logical_and(g >= 1, g < n)))
-            def _():
-                spread_group(g)
-
-            @pl.when(jnp.logical_and(t >= lag, t < lag + n))
-            def _():
-                reduce_group(t - lag)
-
-            return carry
-
-        lax.fori_loop(0, 2 * n, turn, 0)
+        lax.fori_loop(0, 2 * n + 2, turn, 0)
 
         back = rev[span(d * rows, rows)]
         for i in range(1, n):

time: 104 us -> 92.4 us (0.89)
  Pallas kernels: 102 us -> 90.6 us
    pallas_call x1, Pallas kernels: 102 us -> 90.6 us  [body(): pl.pallas_call(functools.partial(kernel, n, layers, tile), out_shape=jax....]
where the time goes in v4:
time: 92.4 us; the launch traced here: 92.2 us
  Pallas kernels  90.6 us (98%)
  local copies, waits for them, and re-layouts  1.59 us (2%)
    pallas_call x1, Pallas kernels, body(): pl.pallas_call(functools.partial(kernel, n, layers, tile), out_shape=jax....  90.6 us

profile of v4, /device:TPU:0, one launch (start us, length us, event | category | flops | bytes accessed | tf_op | source)
XLA Modules:
  0.0 92.2 jit_solution(13006888674482945995)
XLA Ops:
  0.0 90.6 %shard_map.46 = f32[160,256]{1,0:T(8,128)} custom-call(f32[1280,640]{1,0:T(8,128)} %adj.1, f32[160,256]{1,0:T(8,128)} %feat.1, f32[2,2,256,256]{3,2,1,0:T(8,128)} %weights.1, f32[2,256]{1,0:T(2,128)} %biases.1), custom_call_target="tpu_custom_call" | custom-call | flops 5033164800 | bytes 3276800 | tf_op jit(solution)/shard_map/pallas_call | solution.py:372
  90.6 1.6 %copy.6 = f32[160,256]{1,0:T(8,128)} copy(f32[160,256]{1,0:T(8,128)} %shard_map.46) | data formatting | bytes 327680

commit v5 on v4

--- a/solution.py
+++ b/solution.py
@@ -107,49 +107,60 @@
 
         lax.fori_loop(0, tiles, step, 0)
 
+    def gather(l, j):
+        own_rows = xs.at[l, span(d * rows, rows)]
+        return remote(own_rows, own_rows, gs.at[l, j], gr.at[l, n - j], peer(j))
+
+    def place(k):
+        group = lax.rem(d + lax.div(k, SPLIT), n)
+        return group * rows + lax.rem(k, SPLIT) * chunk
+
+    def spread(l, k, to, device):
+        ref = xd.at[l, span(c * half + place(k), chunk)]
+        return remote(ref, ref, zs.at[l, to, k], zr.at[l, k], device)
+
+    def share(l, k):
+        ref = xd.at[l, span(c * half + place(k), chunk)]
+        return remote(ref, ref, cs.at[l, k], cr.at[l, k], mate)
+
+    def spread_group(l, g):
+        for part in range(SPLIT):
+            k = g * SPLIT + part
+
+            @pl.when(root)
+            def _():
+                xd[l, span(c * half + place(k), chunk)] = xs[l, span(place(k), chunk)]
+
+            @pl.when(jnp.logical_not(root))
+            def _():
+                spread(l, k, 0, down).wait_recv()
+
+            @pl.when(below)
+            def _():
+                spread(l, k, 0, down).start()
+
+            @pl.when(above)
+            def _():
+                spread(l, k, 1, up).start()
+
+            share(l, k).start()
+
+    def begin(l):
+        for j in range(1, n):
+            gather(l, j).start()
+
+        @pl.when(root)
+        def _():
+            spread_group(l, 0)
+
+    begin(0)
+    prepare()
+
     for l in range(layers):
-
-        def gather(j):
-            own_rows = xs.at[l, span(d * rows, rows)]
-            return remote(own_rows, own_rows, gs.at[l, j], gr.at[l, n - j], peer(j))
 
         def gathered(i):
             rows_of = xs.at[l, span(lax.rem(d + i, n) * rows, rows)]
             return remote(rows_of, rows_of, gs.at[l, i], gr.at[l, i], peer(i))
-
-        def place(k):
-            group = lax.rem(d + lax.div(k, SPLIT), n)
-            return group * rows + lax.rem(k, SPLIT) * chunk
-
-        def spread(k, to, device):
-            ref = xd.at[l, span(c * half + place(k), chunk)]
-            return remote(ref, ref, zs.at[l, to, k], zr.at[l, k], device)
-
-        def share(k):
-            ref = xd.at[l, span(c * half + place(k), chunk)]
-            return remote(ref, ref, cs.at[l, k], cr.at[l, k], mate)
-
-        def spread_group(g):
-            for part in range(SPLIT):
-                k = g * SPLIT + part
-
-                @pl.when(root)
-                def _():
-                    xd[l, span(c * half + place(k), chunk)] = xs[l, span(place(k), chunk)]
-
-                @pl.when(jnp.logical_not(root))
-                def _():
-                    spread(k, 0, down).wait_recv()
-
-                @pl.when(below)
-                def _():
-                    spread(k, 0, down).start()
-
-                @pl.when(above)
-                def _():
-                    spread(k, 1, up).start()
-
-                share(k).start()
 
         def pair(k):
             span_k = span(k * chunk, chunk)
@@ -202,7 +213,7 @@
 
         def reverse():
             def arrive(k, carry):
-                share(k).wait_recv()
+                share(l, k).wait_recv()
                 return carry
 
             lax.fori_loop(0, chunks, arrive, 0)
@@ -217,22 +228,16 @@
             for j in range(1, n):
                 reverse_out(j).start()
 
-        for j in range(1, n):
-            gather(j).start()
-        for i in range(n):
-            if i > 0:
-                gathered(i).wait_recv()
+        for i in range(1, n):
+            gathered(i).wait_recv()
 
             @pl.when(root)
             def _():
-                spread_group(i)
+                spread_group(l, i)
 
             @pl.when(jnp.logical_and(middle, distance == i))
             def _():
-                spread_group(0)
-
-            if l == 0 and i == 0:
-                prepare()
+                spread_group(l, 0)
 
         x_hi, x_lo = parts_of(xs[l])
         xs_hi[...] = x_hi
@@ -261,7 +266,7 @@
 
             @pl.when(jnp.logical_and(jnp.logical_not(root), jnp.logical_and(g >= first, g < n)))
             def _():
-                spread_group(g)
+                spread_group(l, g)
 
             i = t - reduce_turn
 
@@ -280,33 +285,35 @@
             ).wait_recv()
             back = back + rev_in[l, i]
 
+        mixed = dot3(*parts_of(back), *parts_of(weights[l, 1])) + biases[pl.ds(l, 1)]
+
         @pl.when(jnp.logical_not(root))
         def _():
             total(d).wait_recv()
 
-        mixed = dot3(*parts_of(total_in[l]), *parts_of(weights[l, 0]))
-        mixed = mixed + dot3(*parts_of(back), *parts_of(weights[l, 1]))
-        result = jnp.maximum(mixed + biases[pl.ds(l, 1)], 0.0)
+        mixed = mixed + dot3(*parts_of(total_in[l]), *parts_of(weights[l, 0]))
+        result = jnp.maximum(mixed, 0.0)
         if l + 1 < layers:
             xs[l + 1, span(d * rows, rows)] = result
+            begin(l + 1)
         else:
             out[...] = result
 
         for j in range(1, n):
-            gather(j).wait_send()
+            gather(l, j).wait_send()
             reverse_out(j).wait_send()
 
         def drain(k, carry):
-            share(k).wait_send()
+            share(l, k).wait_send()
             pair(k).wait_send()
 
             @pl.when(below)
             def _():
-                spread(k, 0, down).wait_send()
+                spread(l, k, 0, down).wait_send()
 
             @pl.when(above)
             def _():
-                spread(k, 1, up).wait_send()
+                spread(l, k, 1, up).wait_send()
 
             @pl.when(jnp.logical_not(root))
             def _():

time: 92.4 us -> 92.7 us (level)
  no operation moved by 1% of the time
where the time goes in v5:
time: 92.7 us; the launch traced here: 92.5 us
  Pallas kernels  90.9 us (98%)
  local copies, waits for them, and re-layouts  1.59 us (2%)
    pallas_call x1, Pallas kernels, body(): pl.pallas_call(functools.partial(kernel, n, layers, tile), out_shape=jax....  90.9 us

profile of v5, /device:TPU:0, one launch (start us, length us, event | category | flops | bytes accessed | tf_op | source)
XLA Modules:
  0.0 92.5 jit_solution(18189949260145423992)
XLA Ops:
  0.0 90.9 %shard_map.46 = f32[160,256]{1,0:T(8,128)} custom-call(f32[1280,640]{1,0:T(8,128)} %adj.1, f32[160,256]{1,0:T(8,128)} %feat.1, f32[2,2,256,256]{3,2,1,0:T(8,128)} %weights.1, f32[2,256]{1,0:T(2,128)} %biases.1), custom_call_target="tpu_custom_call" | custom-call | flops 5033164800 | bytes 3276800 | tf_op jit(solution)/shard_map/pallas_call | solution.py:379
  90.9 1.6 %copy.6 = f32[160,256]{1,0:T(8,128)} copy(f32[160,256]{1,0:T(8,128)} %shard_map.46) | data formatting | bytes 327680

commit v6 on v5

--- a/solution.py
+++ b/solution.py
@@ -25,7 +25,7 @@
 def kernel(
     n, layers, tile,
     adj, feat, weights, biases, out,
-    stage, a_hi, a_lo, t_hi, t_lo, xs_hi, xs_lo,
+    stage, a_hi, a_lo, t_hi, t_lo, xs_hi, xs_lo, xd_hi, xd_lo,
     xs, xd, swap_out, own, rev, pair_in, chain_in, rev_in, total_in,
     load_sem, gs, gr, zs, zr, cs, cr, ps, pr, hs, hr, fs, fr, vs, vr,
 ):
@@ -146,8 +146,12 @@
             share(l, k).start()
 
     def begin(l):
-        for j in range(1, n):
-            gather(l, j).start()
+        for m in range(n):
+            j = lax.rem(u + m - d + n, n)
+
+            @pl.when(j != 0)
+            def _():
+                gather(l, j).start()
 
         @pl.when(root)
         def _():
@@ -217,16 +221,25 @@
                 return carry
 
             lax.fori_loop(0, chunks, arrive, 0)
-            rev[...] = jnp.zeros_like(rev)
-
-            def step(t, carry):
-                x_hi, x_lo = parts_of(xd[l, span(t * tile, tile)])
-                rev[...] += dot3(t_hi[t], t_lo[t], x_hi, x_lo)
+            x_hi, x_lo = parts_of(xd[l])
+            xd_hi[...] = x_hi
+            xd_lo[...] = x_lo
+
+            def group(i, carry):
+                rows_of = span(lax.rem(d + 1 + i, n) * rows, rows)
+                total_rows = jnp.zeros((rows, width), jnp.float32)
+                for t in range(tiles):
+                    at = pl.ds(t * tile, tile)
+                    total_rows += dot3(t_hi[t, rows_of], t_lo[t, rows_of], xd_hi[at], xd_lo[at])
+                rev[rows_of] = total_rows
+
+                @pl.when(i < n - 1)
+                def _():
+                    reverse_out(i + 1).start()
+
                 return carry
 
-            lax.fori_loop(0, tiles, step, 0)
-            for j in range(1, n):
-                reverse_out(j).start()
+            lax.fori_loop(0, n, group, 0)
 
         for i in range(1, n):
             gathered(i).wait_recv()
@@ -349,6 +362,8 @@
         vmem((tiles, half, tile), bf16),
         vmem((half, width), bf16),
         vmem((half, width), bf16),
+        vmem((CORES * half, width), bf16),
+        vmem((CORES * half, width), bf16),
         vmem((layers, half, width), f32),
         vmem((layers, CORES * half, width), f32),
         vmem((half, width), f32),

time: 92.7 us -> 87 us (0.939)
  Pallas kernels: 90.9 us -> 85.2 us
    pallas_call x1, Pallas kernels: 90.9 us -> 85.2 us  [body(): pl.pallas_call(functools.partial(kernel, n, layers, tile), out_shape=jax....]
where the time goes in v6:
time: 87 us; the launch traced here: 86.8 us
  Pallas kernels  85.2 us (98%)
  local copies, waits for them, and re-layouts  1.59 us (2%)
    pallas_call x1, Pallas kernels, body(): pl.pallas_call(functools.partial(kernel, n, layers, tile), out_shape=jax....  85.2 us

profile of v6, /device:TPU:0, one launch (start us, length us, event | category | flops | bytes accessed | tf_op | source)
XLA Modules:
  0.0 86.8 jit_solution(3157341375927365781)
XLA Ops:
  0.0 85.2 %shard_map.46 = f32[160,256]{1,0:T(8,128)} custom-call(f32[1280,640]{1,0:T(8,128)} %adj.1, f32[160,256]{1,0:T(8,128)} %feat.1, f32[2,2,256,256]{3,2,1,0:T(8,128)} %weights.1, f32[2,256]{1,0:T(2,128)} %biases.1), custom_call_target="tpu_custom_call" | custom-call | flops 5033164800 | bytes 3276800 | tf_op jit(solution)/shard_map/pallas_call | solution.py:394
  85.2 1.6 %copy.6 = f32[160,256]{1,0:T(8,128)} copy(f32[160,256]{1,0:T(8,128)} %shard_map.46) | data formatting | bytes 327680

commit v7 on v6

--- a/solution.py
+++ b/solution.py
@@ -9,7 +9,7 @@
 
 MESH = pl.DeviceIdType.MESH
 CORES = 2
-SPLIT = 2
+SPLIT = 4
 
 
 def parts_of(value):

time: 87 us -> 87.9 us (1.010)
  Pallas kernels: 85.2 us -> 86.1 us
    pallas_call x1, Pallas kernels: 85.2 us -> 86.1 us  [body(): pl.pallas_call(functools.partial(kernel, n, layers, tile), out_shape=jax....]
where the time goes in v7:
time: 87.9 us; the launch traced here: 87.7 us
  Pallas kernels  86.1 us (98%)
  local copies, waits for them, and re-layouts  1.59 us (2%)
    pallas_call x1, Pallas kernels, body(): pl.pallas_call(functools.partial(kernel, n, layers, tile), out_shape=jax....  86.1 us

profile of v7, /device:TPU:0, one launch (start us, length us, event | category | flops | bytes accessed | tf_op | source)
XLA Modules:
  0.0 87.7 jit_solution(15610329256981101130)
XLA Ops:
  0.0 86.1 %shard_map.46 = f32[160,256]{1,0:T(8,128)} custom-call(f32[1280,640]{1,0:T(8,128)} %adj.1, f32[160,256]{1,0:T(8,128)} %feat.1, f32[2,2,256,256]{3,2,1,0:T(8,128)} %weights.1, f32[2,256]{1,0:T(2,128)} %biases.1), custom_call_target="tpu_custom_call" | custom-call | flops 5033164800 | bytes 3276800 | tf_op jit(solution)/shard_map/pallas_call | solution.py:394
  86.1 1.6 %copy.6 = f32[160,256]{1,0:T(8,128)} copy(f32[160,256]{1,0:T(8,128)} %shard_map.46) | data formatting | bytes 327680

commit v8 on v6

--- a/solution.py
+++ b/solution.py
@@ -45,12 +45,18 @@
     middle = jnp.logical_not(jnp.logical_or(root, tip))
     reverse_turn = jnp.where(tip, 2 * n + 1, n)
     spread_turn = jnp.where(tip, n + 1, 0)
-    reduce_turn = jnp.where(root, n, jnp.where(tip, 1, 1 + reach - distance))
+    reduce_turn = jnp.where(root, 2 * n - 1, jnp.where(tip, 1, 1 + reach - distance))
     mate = {"src": u * CORES + 1 - c, "dst": d}
     down = {"src": s - CORES, "dst": d}
     up = {"src": s + CORES, "dst": d}
     inward = {"src": jnp.where(u < d, s + CORES, s - CORES), "dst": d}
     side = jnp.where(u < d, 0, 1)
+
+    def offset(i):
+        return lax.rem(jnp.where(d < n // 2, i, n - i), n)
+
+    def group_at(i):
+        return lax.rem(d + offset(i), n)
 
     def peer(j):
         return {"src": s, "dst": lax.rem(d + j, n)}
@@ -112,8 +118,7 @@
         return remote(own_rows, own_rows, gs.at[l, j], gr.at[l, n - j], peer(j))
 
     def place(k):
-        group = lax.rem(d + lax.div(k, SPLIT), n)
-        return group * rows + lax.rem(k, SPLIT) * chunk
+        return group_at(lax.div(k, SPLIT)) * rows + lax.rem(k, SPLIT) * chunk
 
     def spread(l, k, to, device):
         ref = xd.at[l, span(c * half + place(k), chunk)]
@@ -182,7 +187,7 @@
             )
 
         def reduce_group(i):
-            r = lax.rem(d + 1 + i, n)
+            r = group_at(n - 1 - i)
             for part in range(SPLIT):
                 k = r * SPLIT + part
                 span_k = span(k * chunk, chunk)
@@ -225,24 +230,20 @@
             xd_hi[...] = x_hi
             xd_lo[...] = x_lo
 
-            def group(i, carry):
-                rows_of = span(lax.rem(d + 1 + i, n) * rows, rows)
-                total_rows = jnp.zeros((rows, width), jnp.float32)
-                for t in range(tiles):
-                    at = pl.ds(t * tile, tile)
-                    total_rows += dot3(t_hi[t, rows_of], t_lo[t, rows_of], xd_hi[at], xd_lo[at])
-                rev[rows_of] = total_rows
-
-                @pl.when(i < n - 1)
-                def _():
-                    reverse_out(i + 1).start()
-
-                return carry
-
-            lax.fori_loop(0, n, group, 0)
+        def reverse_group(i):
+            rows_of = span(group_at(n - 1 - i) * rows, rows)
+            total_rows = jnp.zeros((rows, width), jnp.float32)
+            for t in range(tiles):
+                at = pl.ds(t * tile, tile)
+                total_rows += dot3(t_hi[t, rows_of], t_lo[t, rows_of], xd_hi[at], xd_lo[at])
+            rev[rows_of] = total_rows
+
+            @pl.when(i < n - 1)
+            def _():
+                reverse_out(offset(n - 1 - i)).start()
 
         for i in range(1, n):
-            gathered(i).wait_recv()
+            gathered(offset(i)).wait_recv()
 
             @pl.when(root)
             def _():
@@ -257,11 +258,12 @@
         xs_lo[...] = x_lo
 
         def forward(i):
-            start = lax.rem(d + 1 + i, n) * rows
+            r = group_at(n - 1 - i)
+            start = r * rows
             at = span((1 - c) * half + start, rows)
             swap_out[span(start, rows)] = dot3(a_hi[at], a_lo[at], xs_hi[...], xs_lo[...])
             for part in range(SPLIT):
-                pair(lax.rem(d + 1 + i, n) * SPLIT + part).start()
+                pair(r * SPLIT + part).start()
             at = span(c * half + start, rows)
             own[span(start, rows)] = dot3(a_hi[at], a_lo[at], xs_hi[...], xs_lo[...])
 
@@ -274,6 +276,12 @@
             def _():
                 reverse()
 
+            q = t - reverse_turn
+
+            @pl.when(jnp.logical_and(q >= 0, q < n))
+            def _():
+                reverse_group(q)
+
             g = t - spread_turn
             first = jnp.where(middle, 1, 0)
 
@@ -289,7 +297,7 @@
 
             return carry
 
-        lax.fori_loop(0, 2 * n + 2, turn, 0)
+        lax.fori_loop(0, 3 * n + 1, turn, 0)
 
         back = rev[span(d * rows, rows)]
         for i in range(1, n):

time: 87 us -> 86 us (0.989)
  Pallas kernels: 85.2 us -> 84.2 us
    pallas_call x1, Pallas kernels: 85.2 us -> 84.2 us  [body(): pl.pallas_call(functools.partial(kernel, n, layers, tile), out_shape=jax....]
where the time goes in v8:
time: 86 us; the launch traced here: 85.8 us
  Pallas kernels  84.2 us (98%)
  local copies, waits for them, and re-layouts  1.59 us (2%)
    pallas_call x1, Pallas kernels, body(): pl.pallas_call(functools.partial(kernel, n, layers, tile), out_shape=jax....  84.2 us

profile of v8, /device:TPU:0, one launch (start us, length us, event | category | flops | bytes accessed | tf_op | source)
XLA Modules:
  0.0 85.8 jit_solution(8101118757739998877)
XLA Ops:
  0.0 84.2 %shard_map.46 = f32[160,256]{1,0:T(8,128)} custom-call(f32[1280,640]{1,0:T(8,128)} %adj.1, f32[160,256]{1,0:T(8,128)} %feat.1, f32[2,2,256,256]{3,2,1,0:T(8,128)} %weights.1, f32[2,256]{1,0:T(2,128)} %biases.1), custom_call_target="tpu_custom_call" | custom-call | flops 5033164800 | bytes 3276800 | tf_op jit(solution)/shard_map/pallas_call | solution.py:402
  84.2 1.6 %copy.6 = f32[160,256]{1,0:T(8,128)} copy(f32[160,256]{1,0:T(8,128)} %shard_map.46) | data formatting | bytes 327680

commit v9 on v8

--- a/solution.py
+++ b/solution.py
@@ -101,9 +101,6 @@
             high, low = parts_of(block)
             a_hi[span(t * tile, tile)] = high
             a_lo[span(t * tile, tile)] = low
-            turned_high, turned_low = parts_of(block.T)
-            t_hi[t] = turned_high
-            t_lo[t] = turned_low
 
             @pl.when(t + 2 < tiles)
             def _():
@@ -161,6 +158,14 @@
         @pl.when(root)
         def _():
             spread_group(l, 0)
+
+    def transpose(p):
+        for t in range(0, tiles, n):
+            @pl.when(t + p < tiles)
+            def _():
+                at = span((t + p) * tile, tile)
+                t_hi[t + p] = a_hi[at].T
+                t_lo[t + p] = a_lo[at].T
 
     begin(0)
     prepare()
@@ -271,6 +276,13 @@
             @pl.when(t < n)
             def _():
                 forward(t)
+
+            if l == 0:
+                p = t - jnp.where(tip, n + 1, 0)
+
+                @pl.when(jnp.logical_and(p >= 0, p < n))
+                def _():
+                    transpose(p)
 
             @pl.when(t == reverse_turn)
             def _():

time: 86 us -> 86.5 us (level)
  no operation moved by 1% of the time
where the time goes in v9:
time: 86.5 us; the launch traced here: 86.3 us
  Pallas kernels  84.7 us (98%)
  local copies, waits for them, and re-layouts  1.59 us (2%)
    pallas_call x1, Pallas kernels, body(): pl.pallas_call(functools.partial(kernel, n, layers, tile), out_shape=jax....  84.7 us

profile of v9, /device:TPU:0, one launch (start us, length us, event | category | flops | bytes accessed | tf_op | source)
XLA Modules:
  0.0 86.3 jit_solution(7330766952439650120)
XLA Ops:
  0.0 84.7 %shard_map.46 = f32[160,256]{1,0:T(8,128)} custom-call(f32[1280,640]{1,0:T(8,128)} %adj.1, f32[160,256]{1,0:T(8,128)} %feat.1, f32[2,2,256,256]{3,2,1,0:T(8,128)} %weights.1, f32[2,256]{1,0:T(2,128)} %biases.1), custom_call_target="tpu_custom_call" | custom-call | flops 5033164800 | bytes 3276800 | tf_op jit(solution)/shard_map/pallas_call | solution.py:414
  84.7 1.6 %copy.6 = f32[160,256]{1,0:T(8,128)} copy(f32[160,256]{1,0:T(8,128)} %shard_map.46) | data formatting | bytes 327680

commit v10 on v8

--- a/solution.py
+++ b/solution.py
@@ -44,7 +44,7 @@
     tip = jnp.logical_and(jnp.logical_not(root), distance == reach)
     middle = jnp.logical_not(jnp.logical_or(root, tip))
     reverse_turn = jnp.where(tip, 2 * n + 1, n)
-    spread_turn = jnp.where(tip, n + 1, 0)
+    spread_turn = jnp.where(tip, n + 1, -1)
     reduce_turn = jnp.where(root, 2 * n - 1, jnp.where(tip, 1, 1 + reach - distance))
     mate = {"src": u * CORES + 1 - c, "dst": d}
     down = {"src": s - CORES, "dst": d}

time: 86 us -> 89.9 us (1.045)
  Pallas kernels: 84.2 us -> 88.1 us
    pallas_call x1, Pallas kernels: 84.2 us -> 88.1 us  [body(): pl.pallas_call(functools.partial(kernel, n, layers, tile), out_shape=jax....]
where the time goes in v10:
time: 89.9 us; the launch traced here: 89.7 us
  Pallas kernels  88.1 us (98%)
  local copies, waits for them, and re-layouts  1.59 us (2%)
    pallas_call x1, Pallas kernels, body(): pl.pallas_call(functools.partial(kernel, n, layers, tile), out_shape=jax....  88.1 us

profile of v10, /device:TPU:0, one launch (start us, length us, event | category | flops | bytes accessed | tf_op | source)
XLA Modules:
  0.0 89.7 jit_solution(8460899504254289244)
XLA Ops:
  0.0 88.1 %shard_map.46 = f32[160,256]{1,0:T(8,128)} custom-call(f32[1280,640]{1,0:T(8,128)} %adj.1, f32[160,256]{1,0:T(8,128)} %feat.1, f32[2,2,256,256]{3,2,1,0:T(8,128)} %weights.1, f32[2,256]{1,0:T(2,128)} %biases.1), custom_call_target="tpu_custom_call" | custom-call | flops 5033164800 | bytes 3276800 | tf_op jit(solution)/shard_map/pallas_call | solution.py:402
  88.1 1.6 %copy.6 = f32[160,256]{1,0:T(8,128)} copy(f32[160,256]{1,0:T(8,128)} %shard_map.46) | data formatting | bytes 327680

commit v11 on v10

--- a/solution.py
+++ b/solution.py
@@ -43,8 +43,8 @@
     reach = jnp.where(u < d, d, n - 1 - d)
     tip = jnp.logical_and(jnp.logical_not(root), distance == reach)
     middle = jnp.logical_not(jnp.logical_or(root, tip))
-    reverse_turn = jnp.where(tip, 2 * n + 1, n)
-    spread_turn = jnp.where(tip, n + 1, -1)
+    reverse_turn = jnp.where(tip, 2 * n + 1, jnp.where(middle, n + 1, n))
+    spread_turn = jnp.where(tip, n + 1, jnp.where(middle, 1, 0))
     reduce_turn = jnp.where(root, 2 * n - 1, jnp.where(tip, 1, 1 + reach - distance))
     mate = {"src": u * CORES + 1 - c, "dst": d}
     down = {"src": s - CORES, "dst": d}

time: 89.9 us -> 92.4 us (1.028)
  Pallas kernels: 88.1 us -> 90.5 us
    pallas_call x1, Pallas kernels: 88.1 us -> 90.5 us  [body(): pl.pallas_call(functools.partial(kernel, n, layers, tile), out_shape=jax....]
where the time goes in v11:
time: 92.4 us; the launch traced here: 92.2 us
  Pallas kernels  90.5 us (98%)
  local copies, waits for them, and re-layouts  1.59 us (2%)
    pallas_call x1, Pallas kernels, body(): pl.pallas_call(functools.partial(kernel, n, layers, tile), out_shape=jax....  90.5 us

profile of v11, /device:TPU:0, one launch (start us, length us, event | category | flops | bytes accessed | tf_op | source)
XLA Modules:
  0.0 92.2 jit_solution(13007686754269979086)
XLA Ops:
  0.0 90.5 %shard_map.46 = f32[160,256]{1,0:T(8,128)} custom-call(f32[1280,640]{1,0:T(8,128)} %adj.1, f32[160,256]{1,0:T(8,128)} %feat.1, f32[2,2,256,256]{3,2,1,0:T(8,128)} %weights.1, f32[2,256]{1,0:T(2,128)} %biases.1), custom_call_target="tpu_custom_call" | custom-call | flops 5033164800 | bytes 3276800 | tf_op jit(solution)/shard_map/pallas_call | solution.py:402
  90.6 1.6 %copy.6 = f32[160,256]{1,0:T(8,128)} copy(f32[160,256]{1,0:T(8,128)} %shard_map.46) | data formatting | bytes 327680
